TPU v7x, 256 devices: a whole 4x4x8 slice. The times are simulated.
256 devices in a mesh: wide: 32 (over z, x), narrow: 8 (over y, core).
Axes of the slice: x: 4, y: 4, z: 8, core: 2. Of those that a mesh axis runs over, the one named last changes fastest.
Arguments:
- factor: float32 [131072, 256], P(('wide', 'narrow')), may hold values from -1.5 to 1.5
- quant: bfloat16 [1024, 8, 4, 128, 128], P('wide', 'narrow'), may hold values from -3 to 3
- pattern: int32 [1024, 8, 4], P('wide', 'narrow'), may hold values from 0 to 127, as said below
- exponent: int32 [1024, 8, 4], P('wide', 'narrow'), may hold values from -3 to 1
Outputs:
- stepped: float32 [131072, 256], P(('wide', 'narrow'))
Inputs may be any that keep to these rules, and one draw needn't show every extreme that they name: `pattern`: the 4 column blocks of one block row within one column slab are distinct. Block rows w * 4 * 8 to (w + 1) * 4 * 8 - 1 taken with one column slab n touch, among the column blocks c of that slab with equal c // 4, at most 2 distinct ones, and exactly 2 for some such group.
All inputs are finite; a program needn't handle non-finite values.
Results may differ from a plain program's by a relative error of at most 0.0037.
Values may be sent and summed in bfloat16 or wider, within the bound.
A program may use at most 192 MiB of HBM per device.

v0:
```python
import jax
import jax.numpy as jnp
from jax import lax
from jax.sharding import PartitionSpec as P

step_rate = 0.01


def body(factor, quant, pattern, exponent):
    tile_size = quant.shape[-1]
    rank_width = factor.shape[1]
    own_rows = factor.shape[0]
    blocks_own = own_rows // tile_size
    wide_count = lax.axis_size("wide")
    slab_blocks = blocks_own * wide_count
    compact = factor.astype(jnp.bfloat16)
    row_panel = lax.all_gather(compact, "narrow", axis=0, tiled=True)
    group_rows = row_panel.shape[0] // tile_size
    row_blocks = row_panel.reshape(group_rows, tile_size, rank_width)
    slab_panel = lax.all_gather(compact, "wide", axis=0, tiled=True).reshape(
        slab_blocks, tile_size, rank_width
    )
    chosen = pattern[:, 0, :]
    slot_count = chosen.shape[1]
    column_blocks = slab_panel[chosen]
    scaled = (
        quant[:, 0].astype(jnp.float32)
        * jnp.exp2(exponent[:, 0].astype(jnp.float32))[:, :, None, None]
    )
    predicted = jnp.einsum(
        "bir,btjr->btij", row_blocks, column_blocks, preferred_element_type=jnp.float32
    )
    misfit = (predicted - scaled).astype(jnp.bfloat16)
    row_terms = jnp.einsum(
        "btij,btjr->bir", misfit, column_blocks, preferred_element_type=jnp.float32
    )
    row_terms = row_terms.reshape(group_rows * tile_size, rank_width)
    column_terms = jnp.einsum(
        "btij,bir->btjr", misfit, row_blocks, preferred_element_type=jnp.float32
    )
    dense_grad = jax.ops.segment_sum(
        column_terms.reshape(group_rows * slot_count, tile_size, rank_width),
        chosen.reshape(-1),
        num_segments=slab_blocks,
    )
    dense_grad = dense_grad.reshape(slab_blocks * tile_size, rank_width)
    row_share = lax.psum_scatter(row_terms, "narrow", scatter_dimension=0, tiled=True)
    column_share = lax.psum_scatter(dense_grad, "wide", scatter_dimension=0, tiled=True)
    return factor - step_rate * (row_share + column_share)


def solution(mesh):
    in_specs = (
        P(("wide", "narrow"), None),
        P("wide", "narrow", None, None, None),
        P("wide", "narrow", None),
        P("wide", "narrow", None),
    )
    out_specs = P(("wide", "narrow"), None)
    return jax.shard_map(body, mesh=mesh, in_specs=in_specs, out_specs=out_specs, check_vma=False)
```

profile of v0, /device:TPU:8, one launch (start us, length us, event | category | flops | bytes accessed | tf_op | source)
XLA Modules:
  0.0 472.2 jit_solution(3443612160073938699)
XLA Ops:
  6.5 0.0 all-gather.3.cloned.1.call-start
  6.5 1.8 convert_element_type.20
  8.3 0.0 all-gather.3.cloned.1.call-update
  8.3 0.0 all-gather.5.cloned.1.call-start
  8.4 0.7 all-gather.5.cloned.1.call-update
  9.1 0.0 reduce-scatter.3.cloned.1.call-start
  9.1 0.7 exponential_bitcast_fusion
  9.8 0.1 copy.12
  9.9 0.7 compare_select_fusion
  10.6 0.1 copy.10
  10.7 0.1 reshape.64
  10.8 6.4 %copy.11 = bf16[32,1,4,128,128]{3,4,2,0,1:T(8,128)(2,1)} copy(bf16[32,1,4,128,128]{4,3,2,1,0:T(8,128)(2,1)} %param.5) | data formatting | bytes 8388608 | tf_op args[1]
  17.2 94.0 %all-gather.3.cloned.1.call-done = bf16[16384,256]{1,0:T(8,128)(2,1)} async-done(((bf16[512,256]{1,0:T(8,128)(2,1)}), bf16[16384,256]{1,0:T(8,128)(2,1)}) %all-gather.3.cloned.1.call-update) | async-done | bytes 8388624 | tf_op jit(solution)/shard_map/all_gather | solution.py:20
  111.2 10.0 %gather_fusion = bf16[128,128,256]{2,1,0:T(8,128)(2,1)} fusion(bf16[128,128,256]{2,1,0:T(8,128)(2,1)} %bitcast.46, s32[1024]{0:T(1024)S(1)} %pad_clamp_fusion), kind=kCustom, calls=%fused_computation | custom fusion | bytes 16777728 | tf_op jit(solution)/shard_map/gather | solution.py:25
  121.1 15.8 %all-gather.5.cloned.1.call-done = bf16[4096,256]{1,0:T(8,128)(2,1)} async-done(((bf16[512,256]{1,0:T(8,128)(2,1)}), bf16[4096,256]{1,0:T(8,128)(2,1)}) %all-gather.5.cloned.1.call-update) | async-done | bytes 2097168 | tf_op jit(solution)/shard_map/all_gather | solution.py:17
  137.0 0.0 copy-start
  137.0 9.7 %fusion.10 = f32[32,4,128,128]{3,2,1,0:T(8,128)} fusion(bf16[32,4,128,256]{3,2,1,0:T(8,128)(2,1)} %bitcast.40, bf16[32,128,256,1]{2,1,3,0:T(8,128)(2,1)} %bitcast.44), kind=kOutput, calls=%fused_computation.15 | convolution fusion | flops 1073741824 | bytes 18874368 | tf_op jit(solution)/shard_map/bir,btjr->btij/dot_general | solution.py:30
  146.7 0.0 copy-done
  146.7 0.0 copy-start.3
  146.7 0.0 copy-start.1
  146.7 10.6 %fusion.4 = f32[32,128,256,1]{2,1,3,0:T(8,128)} fusion(bf16[32,4,128,256]{3,2,1,0:T(8,128)(2,1)} %bitcast.41, f32[32,4,128,128]{3,2,1,0:T(8,128)} %fusion.10, bf16[32,1,4,128,128]{3,4,2,0,1:T(8,128)(2,1)S(1)} %copy-done, f32[32,4]{1,0:T(8,128)S(1)} %copy.12), kind=kOutput, calls=%fused_computation.6 | convolution fusion | flops 1082130432 | bytes 25166336 | tf_op jit(solution)/shard_map/btij,btjr->bir/dot_general | solution.py:34
  157.3 0.0 reduce-scatter.3.cloned.1.call-update
  157.3 0.2 reduce-scatter.5.cloned.1.call-start
  157.6 0.0 copy-done.3
  157.6 0.1 copy.14
  157.7 0.1 reshape.72
  157.8 0.0 copy-done.1
  157.8 12.9 %fusion.2 = f32[32,4,128,256]{3,2,1,0:T(8,128)} fusion(bf16[32,128,256,1]{2,1,3,0:T(8,128)(2,1)S(1)} %bitcast.45, f32[32,4,128,128]{3,2,1,0:T(8,128)} %fusion.10, bf16[32,1,4,128,128]{3,4,2,0,1:T(8,128)(2,1)} %copy.11, f32[32,4]{1,0:T(8,128)S(1)} %copy.12), kind=kOutput, calls=%fused_computation.5 | convolution fusion | flops 1082130432 | bytes 31457792 | tf_op jit(solution)/shard_map/btij,bir->btjr/dot_general | solution.py:38
  170.7 8.0 %broadcast_in_dim.2 = f32[128,128,256]{2,1,0:T(8,128)} broadcast(f32[]{:T(128)} %constant.3.clone.1), dimensions={} | broadcast | bytes 16777220 | tf_op jit(solution)/shard_map/broadcast_in_dim | solution.py:41
  178.7 38.9 %scatter_fusion = f32[128,128,256]{2,1,0:T(8,128)} fusion(f32[128,128,256]{2,1,0:T(8,128)} %broadcast_in_dim.2, s32[128]{0:T(128)S(1)} %reshape.72, f32[128,128,256]{2,1,0:T(8,128)} %bitcast.42), kind=kCustom, calls=%fused_computation.1 | custom fusion | flops 4194304 | bytes 50332160 | tf_op jit(solution)/shard_map/scatter-add | solution.py:41
  217.6 0.0 copy-start.2
  217.6 0.0 reduce-scatter.5.cloned.1.call-update
  217.6 0.0 reduce-scatter.3.cloned.1.call-done
  217.6 246.0 %reduce-scatter.5.cloned.1.call-done = f32[512,256]{1,0:T(8,128)} async-done(((f32[16384,256]{1,0:T(8,128)}), f32[512,256]{1,0:T(8,128)}) %reduce-scatter.5.cloned.1.call-update) | async-done | bytes 524304 | tf_op jit(solution)/shard_map/reduce_scatter | solution.py:48
  463.6 0.0 copy-done.2
  463.6 2.1 multiply_subtract_fusion
  (1 shorter events, 0.0 us)
Async XLA Ops:
  6.5 104.6 %all-gather.3.cloned.1.call-start = ((), (), s32[]{:S(2)}) async-start(), calls=%async_computation.2 | async-start | bytes 8650752 | tf_op jit(solution)/shard_map/all_gather | solution.py:20
  8.3 128.6 %all-gather.5.cloned.1.call-start = ((), (), s32[]{:S(2)}) async-start(), calls=%async_computation.3 | async-start | bytes 2359296 | tf_op jit(solution)/shard_map/all_gather | solution.py:17
  9.1 208.5 %reduce-scatter.3.cloned.1.call-start = ((), (), s32[]{:S(2)}) async-start(), calls=%async_computation.4 | async-start | bytes 4718592 | tf_op jit(solution)/shard_map/reduce_scatter | solution.py:47
  137.0 9.7 %copy-start = (bf16[32,1,4,128,128]{3,4,2,0,1:T(8,128)(2,1)S(1)}, bf16[32,1,4,128,128]{3,4,2,0,1:T(8,128)(2,1)}, u32[]{:S(2)}) copy-start(bf16[32,1,4,128,128]{3,4,2,0,1:T(8,128)(2,1)} %copy.11) | copy-start | bytes 12582916
  146.7 10.9 %copy-start.3 = (s32[32,1,4]{0,2,1:T(4,128)S(1)}, s32[32,1,4]{0,2,1:T(4,128)}, u32[]{:S(2)}) copy-start(s32[32,1,4]{0,2,1:T(4,128)} %param.6) | copy-start | bytes 1540
  146.7 11.1 %copy-start.1 = (bf16[4096,256]{1,0:T(8,128)(2,1)S(1)}, bf16[4096,256]{1,0:T(8,128)(2,1)}, u32[]{:S(2)}) copy-start(bf16[4096,256]{1,0:T(8,128)(2,1)} %all-gather.5.cloned.1.call-done) | copy-start | bytes 6291460
  157.3 306.2 %reduce-scatter.5.cloned.1.call-start = ((), (), s32[]{:S(2)}) async-start(), calls=%async_computation.5 | async-start | bytes 17301504 | tf_op jit(solution)/shard_map/reduce_scatter | solution.py:48
  217.6 246.0 %copy-start.2 = (f32[512,256]{1,0:T(8,128)S(1)}, f32[512,256]{1,0:T(8,128)}, u32[]{:S(2)}) copy-start(f32[512,256]{1,0:T(8,128)} %param.4) | copy-start | bytes 1572868
Sparse Core Ops, SparseCore 0:
  9.9 101.1 all-gather.2
  113.0 23.8 all-gather.4
  157.5 38.1 reduce-scatter.2
  217.7 245.8 reduce-scatter.4
where the time goes:
time: 473 us; the launch traced here: 472 us
  waiting for transfers between devices  357 us (75%)
  other arithmetic  44.1 us (9%)
  matrix products  33.2 us (7%)
  local copies, waits for them, and re-layouts  24.9 us (5%)
  between operations  13.2 us (3%)
    reduce_scatter x1, waiting for transfers between devices, body(): lax.psum_scatter(dense_grad, 'wide', scatter_dimension=0, tiled=True)  246 us
    all_gather x1, waiting for transfers between devices, body(): lax.all_gather(compact, 'wide', axis=0, tiled=True)  94 us
    scatter-add x1, other arithmetic, body(): jax.ops.segment_sum(column_terms.reshape(group_rows * slot_count, tile_si...  38.9 us
    all_gather x1, waiting for transfers between devices, body(): row_panel = lax.all_gather(compact, 'narrow', axis=0, tiled=True)  15.8 us
    dot_general x1, matrix products, body(): jnp.einsum('btij,bir->btjr', misfit, row_blocks, preferred_element_type=j...  12.9 us
    dot_general x1, matrix products, body(): jnp.einsum('btij,btjr->bir', misfit, column_blocks, preferred_element_typ...  10.6 us
    gather x1, local copies, waits for them, and re-layouts, body(): column_blocks = slab_panel[chosen]  9.96 us
    dot_general x1, matrix products, body(): jnp.einsum('bir,btjr->btij', row_blocks, column_blocks, preferred_element...  9.71 us
  transfers between devices with their start and end apart: 4, of which 3 were waited for; matrix products, arithmetic and copies ran while one was open for 17% of the time, Pallas kernels for 0%

commit v1 on v0

v1 whole, which is shorter than its diff:
```python
import jax
import jax.numpy as jnp
from jax import lax
from jax.experimental import pallas as pl
from jax.experimental.pallas import tpu as pltpu
from jax.sharding import PartitionSpec as P

step_rate = 0.01

MESH = pl.DeviceIdType.MESH
NX = 4
NZ = 8
NY = 4
NC = 2
BLK = 4
TILE = 128
RANK = 256
GROUP = 32
SLOTS = 64
HALF = 64
NONE = 128
FAR_FIRST = (4, 3, 5, 2, 6, 1, 7, 0)
BF = jnp.bfloat16
F32 = jnp.float32


def index_rows(pattern):
    lane32 = lax.broadcasted_iota(jnp.int32, (GROUP, TILE), 1)
    sub32 = lax.broadcasted_iota(jnp.int32, (GROUP, TILE), 0)
    spread = jnp.zeros((GROUP, TILE), jnp.int32)
    for t in range(4):
        spread = jnp.where((lane32 & 3) == t, jnp.broadcast_to(pattern[:, t : t + 1], (GROUP, TILE)), spread)
    flat = jnp.sum(jnp.where(sub32 == (lane32 >> 2), spread, 0), axis=0, keepdims=True)
    full = (TILE, TILE)
    lane = lax.broadcasted_iota(jnp.int32, full, 1)
    sub = lax.broadcasted_iota(jnp.int32, full, 0)
    across = jnp.broadcast_to(flat, full)
    down = across.T
    prev = jnp.max(jnp.where((across == down) & (sub < lane), sub, -1), axis=0, keepdims=True)
    prev = jnp.where(prev < 0, NONE, prev)
    held_down = jnp.max(jnp.where(across == sub, 1, 0), axis=1, keepdims=True)
    held_across = jnp.max(jnp.where(down == lane, 1, 0), axis=0, keepdims=True)
    before = ((lane >> 2) == (sub >> 2)) & (lane < sub)
    rank = jnp.sum(jnp.where(before, jnp.broadcast_to(held_across, full), 0), axis=1, keepdims=True)
    place = (sub >> 2) * 2 + jnp.broadcast_to(rank, full)
    slot = jnp.sum(jnp.where(across == sub, place, 0), axis=0, keepdims=True)
    wanted = (jnp.broadcast_to(held_down, full) == 1) & (place == lane)
    need = jnp.sum(jnp.where(wanted, sub & 3, 0), axis=0, keepdims=True)
    slot_down = jnp.broadcast_to(slot, full).T
    last = jnp.max(jnp.where(slot_down == lane, sub, -1), axis=0, keepdims=True)
    last = jnp.where(last < 0, NONE, last)
    return slot, prev, last, need


def kernel(
    pattern_ref, expo_ref, fac, quant_hbm, out_ref,
    qraw, qs0, qs1, rowp, panel0, panel1, sums, racc, rsend, rrecv,
    xs0, xs1, cs0, cs1, cr0, cr1, co0, co1, zs0, zs1, zr0, zr1, zown,
    idxv, idxs, nrv, nrs,
    *rest,
):
    zb = (rest[0:8], rest[8:16])
    qsem, isem, n_s, n_r, row_s, row_r, ring_s, ring_r, x_s, x_r, c_s, c_r, z_s, z_r, rr_s, rr_r = rest[16:]
    qs, panel, xs, cs, cr, co, zs, zr = (
        (qs0, qs1), (panel0, panel1), (xs0, xs1), (cs0, cs1), (cr0, cr1), (co0, co1), (zs0, zs1), (zr0, zr1)
    )
    w = lax.axis_index("wide")
    n = lax.axis_index("narrow")
    x, z = lax.rem(w, NX), lax.div(w, NX)
    y, c = lax.div(n, NC), lax.rem(n, NC)

    def x_peer(dx):
        return (z * NX + lax.rem(x + dx, NX), n)

    def z_peer(dz):
        return (lax.rem(z + dz, NZ) * NX + x, n)

    narrow_steps = [(dy, dc) for dy in range(NY) for dc in range(NC) if (dy, dc) != (0, 0)]

    def n_peer(dy, dc):
        return lax.rem(y + dy, NY) * NC + lax.rem(c + dc, NC)

    barrier = pltpu.get_barrier_semaphore()
    peers = [x_peer(d) for d in range(1, NX)] + [z_peer(d) for d in range(1, NZ)]
    peers += [(w, n_peer(*s)) for s in narrow_steps]
    for peer in peers:
        pl.semaphore_signal(barrier, inc=1, device_id=peer, device_id_type=MESH)

    fetch = pltpu.make_async_copy(quant_hbm, qraw, qsem)
    fetch.start()

    rows = index_rows(pattern_ref[...])
    idxv[...] = jnp.zeros((8, TILE), jnp.int32)
    for i, row in enumerate(rows):
        idxv[i : i + 1, :] = row
    spill = pltpu.make_async_copy(idxv, idxs, isem.at[0])
    spill.start()
    for k in range(BLK):
        block = fac[k * TILE : (k + 1) * TILE, :].astype(BF)
        rowp[n * BLK + k] = block
        zb[0][0][k] = block[:HALF]
        zb[1][0][k] = block[HALF:]
    sums[NONE] = jnp.zeros((HALF, RANK), F32)

    pl.semaphore_wait(barrier, len(peers))
    waits = []

    def send(src, dst, s_sem, r_sem, peer):
        copy = pltpu.make_async_remote_copy(
            src_ref=src, dst_ref=dst, send_sem=s_sem, recv_sem=r_sem, device_id=peer, device_id_type=MESH
        )
        copy.start()
        waits.append(copy)
        return copy

    needs = [send(idxv, nrv.at[dx - 1], n_s.at[dx - 1], n_r.at[dx - 1], x_peer(dx)) for dx in range(1, NX)]

    ring = {}

    def ring_send(h, r):
        up_src, up_dst = zb[h][(1 - r) % NZ], zb[h][(-r) % NZ]
        down_src, down_dst = zb[h][r - 1], zb[h][r]
        if r == 4:
            up_src, up_dst = up_src.at[pl.ds(0, 2)], up_dst.at[pl.ds(0, 2)]
            down_src, down_dst = down_src.at[pl.ds(2, 2)], down_dst.at[pl.ds(2, 2)]
        ring[h, r] = (
            send(up_src, up_dst, ring_s.at[h, 0, r - 1], ring_r.at[h, 0, r - 1], z_peer(1)),
            send(down_src, down_dst, ring_s.at[h, 1, r - 1], ring_r.at[h, 1, r - 1], z_peer(NZ - 1)),
        )

    ring_send(0, 1)
    mine = rowp.at[pl.ds(n * BLK, BLK)]
    row_in = [
        send(mine, mine, row_s.at[j], row_r.at[j], (w, n_peer(*s))) for j, s in enumerate(narrow_steps)
    ]
    ring_send(1, 1)

    spill.wait()
    for copy in needs:
        copy.wait_recv()
    spill = pltpu.make_async_copy(nrv, nrs, isem.at[1])
    spill.start()
    spill.wait()

    def owner(d, dx=0):
        return lax.rem(z + d, NZ) * NX + lax.rem(x + dx, NX)

    x_in = {0: [], 1: []}

    def spread_source(h, d):
        source = zb[h][d]
        at = owner(d) * 2
        for dx in (2, 1, 3):
            for r in range(2):
                xs[h][dx - 1, d, r] = source[nrs[NX - 1 - dx, 3, at + r]]
            x_in[h].append(
                send(
                    xs[h].at[dx - 1, d], panel[h].at[pl.ds(at, 2)],
                    x_s.at[h, dx - 1, d], x_r.at[h, dx - 1, d], x_peer(dx),
                )
            )
        for r in range(2):
            panel[h][at + r] = source[idxs[3, at + r]]

    for h in range(2):
        spread_source(h, 0)
        for r in range(1, 5):
            for copy in ring[h, r]:
                copy.wait_recv()
            if r < 4:
                ring_send(h, r + 1)
            spread_source(h, (-r) % NZ)
            if r < 4:
                spread_source(h, r)

    fetch.wait()
    low = lax.broadcasted_iota(jnp.int32, (TILE, TILE), 1) < HALF

    def scale_row(b, carry):
        for pair in range(2):
            parts = []
            for t in (2 * pair, 2 * pair + 1):
                grow = lax.shift_left(1, expo_ref[b, t] + 3).astype(F32) * 0.125
                parts.append(qraw[b, 0, t].astype(F32) * grow)
            a, b2 = parts
            qs0[b, pair] = jnp.where(low, a, pltpu.roll(b2, HALF, 1)).astype(BF)
            qs1[b, pair] = jnp.where(low, pltpu.roll(a, HALF, 1), b2).astype(BF)
        return carry

    lax.fori_loop(0, GROUP, scale_row, 0)

    for copy in row_in:
        copy.wait_recv()

    def compute(h):
        def step(b, carry):
            mine = rowp[b]
            cols = jnp.concatenate([panel[h][idxs[0, b * 4 + t]] for t in range(4)], axis=0)
            pred = lax.dot_general(mine, cols, (((1,), (1,)), ((), ())), preferred_element_type=F32)
            scaled = jnp.concatenate([qs[h][b, 0], qs[h][b, 1]], axis=1).astype(F32)
            misfit = (pred - scaled).astype(BF)
            row = jnp.dot(misfit, cols, preferred_element_type=F32)
            if h == 0:
                racc[b] = row
            else:
                row = row + racc[b]
                racc[b] = row
                rsend[b] = row.astype(BF)
            term = lax.dot_general(misfit, mine, (((0,), (0,)), ((), ())), preferred_element_type=F32)
            for t in range(4):
                i = b * 4 + t
                sums[i] = term[t * HALF : (t + 1) * HALF] + sums[idxs[1, i]]
            return carry

        lax.fori_loop(0, GROUP, step, 0)

    c_in = {}

    def send_terms(h):
        for d in FAR_FIRST:
            for dx in (2, 1, 3):
                at = owner(d, dx) * 2
                for r in range(2):
                    cs[h][dx - 1, d, r] = sums[idxs[2, at + r]].astype(BF)
                c_in[h, d, dx] = send(
                    cs[h].at[dx - 1, d], cr[h].at[dx - 1, d],
                    c_s.at[h, dx - 1, d], c_r.at[h, dx - 1, d], x_peer(dx),
                )
            at = owner(d) * 2
            for r in range(2):
                co[h][d, r] = sums[idxs[2, at + r]]

    for copy in x_in[0]:
        copy.wait_recv()
    compute(0)
    send_terms(0)
    for copy in x_in[1]:
        copy.wait_recv()
    compute(1)
    r_in = [
        send(
            rsend.at[pl.ds(n_peer(*s) * BLK, BLK)], rrecv.at[j], rr_s.at[j], rr_r.at[j], (w, n_peer(*s))
        )
        for j, s in enumerate(narrow_steps)
    ]
    send_terms(1)

    z_in = []
    for h in range(2):
        for d in FAR_FIRST:
            for dx in range(1, NX):
                c_in[h, d, dx].wait_recv()
            at = owner(d) * 2
            marks = []
            for source in range(4):
                for r in range(2):
                    place = idxs[3, at + r] if source == 3 else nrs[source, 3, at + r]
                    marks.append([jnp.where(place == k, 1.0, 0.0).astype(F32) for k in range(BLK)])

            def strip(i, carry, h=h, d=d, marks=marks):
                span = pl.ds(pl.multiple_of(i * 16, 16), 16)
                terms = []
                for source in range(4):
                    for r in range(2):
                        if source == 3:
                            terms.append(co[h][d, r, span, :])
                        else:
                            terms.append(cr[h][source, d, r, span, :].astype(F32))
                for k in range(BLK):
                    total = terms[0] * marks[0][k]
                    for term, mark in zip(terms[1:], marks[1:]):
                        total = total + term * mark[k]
                    if d == 0:
                        zown[h, k, span, :] = total
                    else:
                        zs[h][d - 1, k, span, :] = total.astype(BF)
                return carry

            lax.fori_loop(0, HALF // 16, strip, 0)
            if d != 0:
                z_in.append(
                    send(zs[h].at[d - 1], zr[h].at[d - 1], z_s.at[h, d - 1], z_r.at[h, d - 1], z_peer(d))
                )

    for copy in r_in:
        copy.wait_recv()
    for copy in z_in:
        copy.wait_recv()
    for h in range(2):
        for k in range(BLK):
            def finish(i, carry, h=h, k=k):
                span = pl.ds(pl.multiple_of(i * 16, 16), 16)
                inner = pl.ds(pl.multiple_of(h * HALF + i * 16, 16), 16)
                outer = pl.ds(pl.multiple_of(k * TILE + h * HALF + i * 16, 16), 16)
                total = zown[h, k, span, :] + racc[n * BLK + k, inner, :]
                for j in range(7):
                    total = total + zr[h][j, k, span, :].astype(F32)
                    total = total + rrecv[j, k, inner, :].astype(F32)
                out_ref[outer, :] = fac[outer, :] - step_rate * total
                return carry

            lax.fori_loop(0, HALF // 16, finish, 0)
    for copy in waits:
        copy.wait_send()


def body(factor, quant, pattern, exponent):
    vmem = pl.BlockSpec(memory_space=pltpu.VMEM)
    smem = pl.BlockSpec(memory_space=pltpu.SMEM)
    dma = pltpu.SemaphoreType.DMA
    V = pltpu.VMEM
    scratch = [
        V((GROUP, 1, 4, TILE, TILE), BF),
        V((GROUP, 2, TILE, TILE), BF), V((GROUP, 2, TILE, TILE), BF),
        V((GROUP, TILE, RANK), BF),
        V((SLOTS, HALF, RANK), BF), V((SLOTS, HALF, RANK), BF),
        V((NONE + 1, HALF, RANK), F32),
        V((GROUP, TILE, RANK), F32),
        V((GROUP, TILE, RANK), BF),
        V((7, BLK, TILE, RANK), BF),
    ]
    scratch += [V((3, NZ, 2, HALF, RANK), BF)] * 6
    scratch += [V((NZ, 2, HALF, RANK), F32)] * 2
    scratch += [V((7, BLK, HALF, RANK), BF)] * 4
    scratch += [V((2, BLK, HALF, RANK), F32)]
    scratch += [
        V((8, TILE), jnp.int32), pltpu.SMEM((8, TILE), jnp.int32),
        V((3, 8, TILE), jnp.int32), pltpu.SMEM((3, 8, TILE), jnp.int32),
    ]
    scratch += [V((BLK, HALF, RANK), BF)] * 16
    scratch += [
        dma, dma((2,)), dma((3,)), dma((3,)), dma((7,)), dma((7,)), dma((2, 2, 4)), dma((2, 2, 4)),
        dma((2, 3, NZ)), dma((2, 3, NZ)), dma((2, 3, NZ)), dma((2, 3, NZ)), dma((2, 7)), dma((2, 7)),
        dma((7,)), dma((7,)),
    ]
    return pl.pallas_call(
        kernel,
        out_shape=jax.ShapeDtypeStruct(factor.shape, factor.dtype),
        in_specs=[vmem, smem, vmem, pl.BlockSpec(memory_space=pl.ANY)],
        out_specs=vmem,
        scratch_shapes=scratch,
        compiler_params=pltpu.CompilerParams(
            collective_id=0, has_side_effects=True, vmem_limit_bytes=58 * 1024 * 1024
        ),
        cost_estimate=pl.CostEstimate(flops=3_300_000_000, bytes_accessed=6_000_000, transcendentals=0),
        name="completion_step",
    )(pattern[:, 0, :], exponent[:, 0, :], factor, quant)


def solution(mesh):
    in_specs = (
        P(("wide", "narrow"), None),
        P("wide", "narrow", None, None, None),
        P("wide", "narrow", None),
        P("wide", "narrow", None),
    )
    out_specs = P(("wide", "narrow"), None)
    return jax.shard_map(body, mesh=mesh, in_specs=in_specs, out_specs=out_specs, check_vma=False)
```

time: 473 us -> 132 us (0.28)
  waiting for transfers between devices: 357 us -> 0 us
  Pallas kernels: 0 us -> 125 us
  other arithmetic: 44.1 us -> 0 us
  matrix products: 33.2 us -> 0 us
  local copies, waits for them, and re-layouts: 24.9 us -> 4.59 us
  between operations: 13.2 us -> 0.01 us
    reduce_scatter x2 -> x0, waiting for transfers between devices: 246 us -> none  [the longest x1 246 us: body(): lax.psum_scatter(dense_grad, 'wide', scatter_dimension=0, tiled=True)]
    pallas_call x0 -> x1, Pallas kernels: none -> 125 us  [body(): pl.pallas_call(kernel, out_shape=jax.ShapeDtypeStruct(factor.shape, facto...]
    all_gather x2 -> x0, waiting for transfers between devices: 110 us -> none  [the longest x1 94 us: body(): lax.all_gather(compact, 'wide', axis=0, tiled=True)]
    scatter-add x1 -> x0, other arithmetic: 38.9 us -> none  [body(): jax.ops.segment_sum(column_terms.reshape(group_rows * slot_count, tile_si...]
    dot_general x3 -> x0, matrix products: 33.2 us -> none  [the longest x1 12.9 us: body(): jnp.einsum('btij,bir->btjr', misfit, row_blocks, preferred_element_type=j...]
    gather x1 -> x0, local copies, waits for them, and re-layouts: 9.96 us -> none  [body(): column_blocks = slab_panel[chosen]]
    broadcast_in_dim x1 -> x0, local copies, waits for them, and re-layouts: 7.99 us -> none  [body(): jax.ops.segment_sum(column_terms.reshape(group_rows * slot_count, tile_si...]
  transfers between devices with their start and end apart: 4 -> 0, of which waited for: 3 -> 0; matrix products, arithmetic and copies ran while one was open for 17% -> 0% of each run, Pallas kernels for 0% -> 0%
where the time goes in v1:
time: 132 us; the launch traced here: 130 us
  Pallas kernels  125 us (95%)
  local copies, waits for them, and re-layouts  4.59 us (3%)
    pallas_call x1, Pallas kernels, body(): pl.pallas_call(kernel, out_shape=jax.ShapeDtypeStruct(factor.shape, facto...  125 us

profile of v1, /device:TPU:8, one launch (start us, length us, event | category | flops | bytes accessed | tf_op | source)
XLA Modules:
  0.0 129.8 jit_solution(1389770077745354699)
XLA Ops:
  0.0 1.4 %copy.5.pattern_ref = s32[32,4]{1,0:T(8,128)} copy(s32[32,4]{0,1:T(4,128)} %bitcast.2) | data formatting | bytes 1024 | tf_op jit(solution)/shard_map/squeeze | solution.py:347
  1.4 1.4 %copy.6.expo_ref = s32[32,4]{1,0:T(8,128)} copy(s32[32,4]{0,1:T(4,128)} %bitcast.3) | data formatting | bytes 1024 | tf_op jit(solution)/shard_map/squeeze | solution.py:347
  2.7 125.2 %completion_step.1 = f32[512,256]{1,0:T(8,128)} custom-call(s32[32,4]{1,0:T(8,128)} %copy.5.pattern_ref, s32[32,4]{1,0:T(8,128)} %copy.6.expo_ref, f32[512,256]{1,0:T(8,128)} %fac.1, bf16[32,1,4,128,128]{4,3,2,1,0:T(8,128)(2,1)} %quant_hbm.1), custom_call_target="tpu_custom_call" | custom-call | flops 3300000000 | bytes 6000000 | tf_op jit(solution)/shard_map/completion_step/pallas_call | solution.py:336
  127.9 1.9 %copy.8 = f32[512,256]{1,0:T(8,128)} copy(f32[512,256]{1,0:T(8,128)} %completion_step.1) | data formatting | bytes 1048576

commit v2 on v1

v2 whole, which is shorter than its diff:
```python
import jax
import jax.numpy as jnp
from jax import lax
from jax.experimental import pallas as pl
from jax.experimental.pallas import tpu as pltpu
from jax.sharding import PartitionSpec as P

step_rate = 0.01

MESH = pl.DeviceIdType.MESH
NX = 4
NZ = 8
NY = 4
NC = 2
BLK = 4
TILE = 128
RANK = 256
GROUP = 32
SLOTS = 64
HALF = 64
NONE = 128
FAR_FIRST = (4, 3, 5, 2, 6, 1, 7, 0)
OVER_Z = {1: (1, 7), 2: (1, 7, 2, 6), 3: (1, 7)}
NEAR_Z = (1, 7, 2, 6)
MESSAGES = 160
LATE = 4
RING1, DENSE1, ZS = 2, 4, 3
BF = jnp.bfloat16
F32 = jnp.float32


def index_rows(pattern):
    lane32 = lax.broadcasted_iota(jnp.int32, (GROUP, TILE), 1)
    sub32 = lax.broadcasted_iota(jnp.int32, (GROUP, TILE), 0)
    spread = jnp.zeros((GROUP, TILE), jnp.int32)
    for t in range(4):
        spread = jnp.where((lane32 & 3) == t, jnp.broadcast_to(pattern[:, t : t + 1], (GROUP, TILE)), spread)
    flat = jnp.sum(jnp.where(sub32 == (lane32 >> 2), spread, 0), axis=0, keepdims=True)
    full = (TILE, TILE)
    lane = lax.broadcasted_iota(jnp.int32, full, 1)
    sub = lax.broadcasted_iota(jnp.int32, full, 0)
    across = jnp.broadcast_to(flat, full)
    down = across.T
    prev = jnp.max(jnp.where((across == down) & (sub < lane), sub, -1), axis=0, keepdims=True)
    prev = jnp.where(prev < 0, NONE, prev)
    held_down = jnp.max(jnp.where(across == sub, 1, 0), axis=1, keepdims=True)
    held_across = jnp.max(jnp.where(down == lane, 1, 0), axis=0, keepdims=True)
    before = ((lane >> 2) == (sub >> 2)) & (lane < sub)
    rank = jnp.sum(jnp.where(before, jnp.broadcast_to(held_across, full), 0), axis=1, keepdims=True)
    place = (sub >> 2) * 2 + jnp.broadcast_to(rank, full)
    slot = jnp.sum(jnp.where(across == sub, place, 0), axis=0, keepdims=True)
    wanted = (jnp.broadcast_to(held_down, full) == 1) & (place == lane)
    need = jnp.sum(jnp.where(wanted, sub & 3, 0), axis=0, keepdims=True)
    slot_down = jnp.broadcast_to(slot, full).T
    last = jnp.max(jnp.where(slot_down == lane, sub, -1), axis=0, keepdims=True)
    last = jnp.where(last < 0, NONE, last)
    return slot, prev, last, need


def kernel(
    pattern_ref, expo_ref, fac, quant_hbm, out_ref,
    qraw, qs0, qs1, rowp, panel0, panel1, sums, racc, rsend, rrecv,
    xs0, xs1, zp0, zp1, cs0, cs1, cr0, cr1, co0, co1, zs0, zs1, zr0, zr1, zown,
    idxv, idxs, nrv, nrs,
    *rest,
):
    zb = (rest[0:8], rest[8:16])
    xd = (rest[16:19], rest[19:22])
    qsem, isem, send_sem, recv_sem = rest[22:]
    qs, panel, xs, zp = (qs0, qs1), (panel0, panel1), (xs0, xs1), (zp0, zp1)
    cs, cr, co, zs, zr = (cs0, cs1), (cr0, cr1), (co0, co1), (zs0, zs1), (zr0, zr1)
    w = lax.axis_index("wide")
    n = lax.axis_index("narrow")
    x, z = lax.rem(w, NX), lax.div(w, NX)
    y, c = lax.div(n, NC), lax.rem(n, NC)

    def x_peer(dx):
        return (z * NX + lax.rem(x + dx, NX), n)

    def z_peer(dz):
        return (lax.rem(z + dz, NZ) * NX + x, n)

    narrow_steps = [(dy, dc) for dy in range(NY) for dc in range(NC) if (dy, dc) != (0, 0)]

    def n_peer(dy, dc):
        return lax.rem(y + dy, NY) * NC + lax.rem(c + dc, NC)

    barrier = pltpu.get_barrier_semaphore()
    peers = [x_peer(d) for d in range(1, NX)] + [z_peer(d) for d in range(1, NZ)]
    peers += [(w, n_peer(*s)) for s in narrow_steps]
    for peer in peers:
        pl.semaphore_signal(barrier, inc=1, device_id=peer, device_id_type=MESH)

    fetch = pltpu.make_async_copy(quant_hbm, qraw, qsem)
    fetch.start()

    for k in range(BLK):
        block = fac[k * TILE : (k + 1) * TILE, :].astype(BF)
        rowp[n * BLK + k] = block
        zb[0][0][k] = block[:HALF]
        zb[1][0][k] = block[HALF:]
    idxv[...] = jnp.zeros((8, TILE), jnp.int32)
    idxv[0:4, 0:GROUP] = pattern_ref[...]
    rows = index_rows(idxv[...].T[:GROUP, :4])
    for i, row in enumerate(rows):
        idxv[i : i + 1, :] = row
    spill = pltpu.make_async_copy(idxv, idxs, isem.at[0])
    spill.start()
    sums[NONE] = jnp.zeros((HALF, RANK), F32)

    pl.semaphore_wait(barrier, len(peers))
    sent = []
    used = iter(range(MESSAGES))

    def send(src, dst, peer):
        i = next(used)
        copy = pltpu.make_async_remote_copy(
            src_ref=src, dst_ref=dst, send_sem=send_sem.at[i], recv_sem=recv_sem.at[i],
            device_id=peer, device_id_type=MESH,
        )
        copy.start()
        sent.append(copy)
        return copy

    def settle():
        while sent:
            sent.pop().wait_send()

    ring = {}

    def ring_send(h, r):
        up_src, up_dst = zb[h][(1 - r) % NZ], zb[h][(-r) % NZ]
        down_src, down_dst = zb[h][r - 1], zb[h][r]
        if r == 4:
            up_src, up_dst = up_src.at[pl.ds(0, 2)], up_dst.at[pl.ds(0, 2)]
            down_src, down_dst = down_src.at[pl.ds(2, 2)], down_dst.at[pl.ds(2, 2)]
        ring[h, r] = (send(up_src, up_dst, z_peer(1)), send(down_src, down_dst, z_peer(NZ - 1)))

    dense = {}

    def dense_send(h):
        for dx in (2, 1, 3):
            dense[h, dx] = send(zb[h][0], xd[h][dx - 1], x_peer(dx))

    needs, of_x, of_z = [], {}, {}
    for dx in range(1, NX):
        of_x[NX - dx] = len(needs)
        needs.append(send(idxv, nrv.at[len(needs)], x_peer(dx)))
    for dz in NEAR_Z:
        of_z[NZ - dz] = len(needs)
        needs.append(send(idxv, nrv.at[len(needs)], z_peer(dz)))
    ring_send(0, 1)
    dense_send(0)
    mine = rowp.at[pl.ds(n * BLK, BLK)]
    row_in = [send(mine, mine, (w, n_peer(*s))) for s in narrow_steps]

    def owner(d, dx=0):
        return lax.rem(z + d, NZ) * NX + lax.rem(x + dx, NX)

    panel_in = {0: [], 1: []}

    def keep(h, source, at):
        for r in range(2):
            panel[h][at + r] = source[idxs[3, at + r]]

    def spread_along_z(h):
        place = 0
        for dx in (2, 1, 3):
            dense[h, dx].wait_recv()
            source = xd[h][dx - 1]
            at = owner(0, NX - dx) * 2
            for dz in NEAR_Z:
                if NZ - dz not in OVER_Z[dx]:
                    continue
                for r in range(2):
                    zp[h][place, r] = source[nrs[of_z[dz], 3, at + r]]
                panel_in[h].append(send(zp[h].at[place], panel[h].at[pl.ds(at, 2)], z_peer(dz)))
                place += 1
            keep(h, source, at)

    places = {0: 0, 1: 0}

    def spread_along_x(h, d):
        source = zb[h][d]
        at = owner(d) * 2
        for dx in (2, 1, 3):
            if d == 0 or d in OVER_Z[dx]:
                continue
            for r in range(2):
                xs[h][places[h], r] = source[nrs[of_x[dx], 3, at + r]]
            panel_in[h].append(send(xs[h].at[places[h]], panel[h].at[pl.ds(at, 2)], x_peer(dx)))
            places[h] += 1
        keep(h, source, at)

    spill.wait()
    for copy in needs:
        copy.wait_recv()
    spill = pltpu.make_async_copy(nrv, nrs, isem.at[1])
    spill.start()
    spill.wait()

    for h in range(2):
        for r in range(1, 5):
            for copy in ring[h, r]:
                copy.wait_recv()
            if r < 4:
                ring_send(h, r + 1)
            if r == RING1 and h == 0:
                ring_send(1, 1)
            spread_along_x(h, (-r) % NZ)
            if r < 4:
                spread_along_x(h, r)
            if r == DENSE1 and h == 0:
                dense_send(1)
            if r == ZS and r < 4:
                spread_along_z(h)
        spread_along_x(h, 0)
        if ZS == 4:
            spread_along_z(h)

    fetch.wait()
    low = lax.broadcasted_iota(jnp.int32, (TILE, TILE), 1) < HALF

    def scale_row(b, carry):
        for pair in range(2):
            parts = []
            for t in (2 * pair, 2 * pair + 1):
                grow = lax.shift_left(1, expo_ref[t, b] + 3).astype(F32) * 0.125
                parts.append(qraw[b, 0, t].astype(F32) * grow)
            first, second = parts
            qs0[b, pair] = jnp.where(low, first, pltpu.roll(second, HALF, 1)).astype(BF)
            qs1[b, pair] = jnp.where(low, pltpu.roll(first, HALF, 1), second).astype(BF)
        return carry

    lax.fori_loop(0, GROUP, scale_row, 0)

    for copy in row_in:
        copy.wait_recv()

    def compute(h, low_row, high_row):
        def step(b, carry):
            mine = rowp[b]
            cols = jnp.concatenate([panel[h][idxs[0, b * 4 + t]] for t in range(4)], axis=0)
            pred = lax.dot_general(mine, cols, (((1,), (1,)), ((), ())), preferred_element_type=F32)
            scaled = jnp.concatenate([qs[h][b, 0], qs[h][b, 1]], axis=1).astype(F32)
            misfit = (pred - scaled).astype(BF)
            row = jnp.dot(misfit, cols, preferred_element_type=F32)
            if h == 0:
                racc[b] = row
            else:
                row = row + racc[b]
                racc[b] = row
                rsend[b] = row.astype(BF)
            term = lax.dot_general(misfit, mine, (((0,), (0,)), ((), ())), preferred_element_type=F32)
            for t in range(4):
                i = b * 4 + t
                sums[i] = term[t * HALF : (t + 1) * HALF] + sums[idxs[1, i]]
            return carry

        lax.fori_loop(low_row, high_row, step, 0, unroll=4)

    terms_in = {}

    def send_terms(h):
        for d in FAR_FIRST:
            for dx in (2, 1, 3):
                at = owner(d, dx) * 2
                for r in range(2):
                    cs[h][dx - 1, d, r] = sums[idxs[2, at + r]].astype(BF)
                terms_in[h, d, dx] = send(cs[h].at[dx - 1, d], cr[h].at[dx - 1, d], x_peer(dx))
            at = owner(d) * 2
            for r in range(2):
                co[h][d, r] = sums[idxs[2, at + r]]

    z_in = {0: [], 1: []}

    def add_terms(h, d):
        for dx in range(1, NX):
            terms_in[h, d, dx].wait_recv()
        at = owner(d) * 2
        marks = []
        for source in range(4):
            for r in range(2):
                place = idxs[3, at + r] if source == 0 else nrs[of_x[NX - source], 3, at + r]
                marks.append([jnp.where(place == k, 1.0, 0.0).astype(F32) for k in range(BLK)])

        def strip(i, carry):
            span = pl.ds(pl.multiple_of(i * 16, 16), 16)
            terms = [co[h][d, r, span, :] for r in range(2)]
            terms += [cr[h][source, d, r, span, :].astype(F32) for source in range(3) for r in range(2)]
            for k in range(BLK):
                total = terms[0] * marks[0][k]
                for term, mark in zip(terms[1:], marks[1:]):
                    total = total + term * mark[k]
                if d == 0:
                    zown[h, k, span, :] = total
                else:
                    zs[h][d - 1, k, span, :] = total.astype(BF)
            return carry

        lax.fori_loop(0, HALF // 16, strip, 0)
        if d != 0:
            z_in[h].append(send(zs[h].at[d - 1], zr[h].at[d - 1], z_peer(d)))

    for copy in panel_in[0]:
        copy.wait_recv()
    compute(0, 0, GROUP)
    send_terms(0)
    for copy in panel_in[1]:
        copy.wait_recv()
    early = len(FAR_FIRST) - LATE
    for part in range(4):
        compute(1, part * 8, part * 8 + 8)
        if part >= 4 - early:
            add_terms(0, FAR_FIRST[part - 4 + early])
    send_terms(1)
    r_in = [
        send(rsend.at[pl.ds(n_peer(*s) * BLK, BLK)], rrecv.at[j], (w, n_peer(*s)))
        for j, s in enumerate(narrow_steps)
    ]
    for d in FAR_FIRST[early:]:
        add_terms(0, d)
    for d in FAR_FIRST[:-3]:
        add_terms(1, d)
    for copy in r_in:
        copy.wait_recv()
    settled = sent[-3:]
    del sent[-3:]
    settle()
    sent.extend(settled)

    def base(i, carry):
        for k in range(BLK):
            inner = pl.ds(pl.multiple_of(i * 16, 16), 16)
            outer = pl.ds(pl.multiple_of(k * TILE + i * 16, 16), 16)
            total = racc[n * BLK + k, inner, :]
            for j in range(7):
                total = total + rrecv[j, k, inner, :].astype(F32)
            out_ref[outer, :] = fac[outer, :] - step_rate * total
        return carry

    lax.fori_loop(0, TILE // 16, base, 0)
    for d in FAR_FIRST[-3:]:
        add_terms(1, d)

    def finish(h):
        def strip(i, carry):
            for k in range(BLK):
                span = pl.ds(pl.multiple_of(i * 16, 16), 16)
                outer = pl.ds(pl.multiple_of(k * TILE + h * HALF + i * 16, 16), 16)
                total = zown[h, k, span, :]
                for j in range(7):
                    total = total + zr[h][j, k, span, :].astype(F32)
                out_ref[outer, :] = out_ref[outer, :] - step_rate * total
            return carry

        for copy in z_in[h]:
            copy.wait_recv()
        lax.fori_loop(0, HALF // 16, strip, 0)

    finish(0)
    finish(1)
    settle()


def body(factor, quant, pattern, exponent):
    vmem = pl.BlockSpec(memory_space=pltpu.VMEM)
    smem = pl.BlockSpec(memory_space=pltpu.SMEM)
    dma = pltpu.SemaphoreType.DMA
    V = pltpu.VMEM
    scratch = [
        V((GROUP, 1, 4, TILE, TILE), BF),
        V((GROUP, 2, TILE, TILE), BF), V((GROUP, 2, TILE, TILE), BF),
        V((GROUP, TILE, RANK), BF),
        V((SLOTS, HALF, RANK), BF), V((SLOTS, HALF, RANK), BF),
        V((NONE + 1, HALF, RANK), F32),
        V((GROUP, TILE, RANK), F32),
        V((GROUP, TILE, RANK), BF),
        V((7, BLK, TILE, RANK), BF),
    ]
    scratch += [V((13, 2, HALF, RANK), BF)] * 2
    scratch += [V((8, 2, HALF, RANK), BF)] * 2
    scratch += [V((3, NZ, 2, HALF, RANK), BF)] * 4
    scratch += [V((NZ, 2, HALF, RANK), F32)] * 2
    scratch += [V((7, BLK, HALF, RANK), BF)] * 4
    scratch += [V((2, BLK, HALF, RANK), F32)]
    scratch += [
        V((8, TILE), jnp.int32), pltpu.SMEM((8, TILE), jnp.int32),
        V((7, 8, TILE), jnp.int32), pltpu.SMEM((7, 8, TILE), jnp.int32),
    ]
    scratch += [V((BLK, HALF, RANK), BF)] * 22
    scratch += [dma, dma((2,)), dma((MESSAGES,)), dma((MESSAGES,))]
    return pl.pallas_call(
        kernel,
        out_shape=jax.ShapeDtypeStruct(factor.shape, factor.dtype),
        in_specs=[vmem, smem, vmem, pl.BlockSpec(memory_space=pl.ANY)],
        out_specs=vmem,
        scratch_shapes=scratch,
        compiler_params=pltpu.CompilerParams(
            collective_id=0, has_side_effects=True, vmem_limit_bytes=58 * 1024 * 1024
        ),
        cost_estimate=pl.CostEstimate(flops=3_300_000_000, bytes_accessed=6_000_000, transcendentals=0),
        name="completion_step",
    )(pattern[:, 0, :].T, exponent[:, 0, :].T, factor, quant)


def solution(mesh):
    in_specs = (
        P(("wide", "narrow"), None),
        P("wide", "narrow", None, None, None),
        P("wide", "narrow", None),
        P("wide", "narrow", None),
    )
    out_specs = P(("wide", "narrow"), None)
    return jax.shard_map(body, mesh=mesh, in_specs=in_specs, out_specs=out_specs, check_vma=False)
```

time: 132 us -> 115 us (0.87)
  Pallas kernels: 125 us -> 112 us
  local copies, waits for them, and re-layouts: 4.59 us -> 1.87 us
    pallas_call x1, Pallas kernels: 125 us -> 112 us  [body(): pl.pallas_call(kernel, out_shape=jax.ShapeDtypeStruct(factor.shape, facto...]
    squeeze x2 -> x0, local copies, waits for them, and re-layouts: 2.72 us -> none  [the longest x1 1.37 us: body(): pattern[:, 0, :]]
where the time goes in v2:
time: 115 us; the launch traced here: 114 us
  Pallas kernels  112 us (97%)
  local copies, waits for them, and re-layouts  1.87 us (2%)
    pallas_call x1, Pallas kernels, body(): pl.pallas_call(kernel, out_shape=jax.ShapeDtypeStruct(factor.shape, facto...  112 us

profile of v2, /device:TPU:8, one launch (start us, length us, event | category | flops | bytes accessed | tf_op | source)
XLA Modules:
  0.0 113.8 jit_solution(1667010975881432504)
XLA Ops:
  0.0 111.9 %completion_step.1 = f32[512,256]{1,0:T(8,128)} custom-call(s32[4,32]{1,0:T(4,128)} %bitcast.6, s32[4,32]{1,0:T(4,128)} %bitcast.7, f32[512,256]{1,0:T(8,128)} %fac.1, bf16[32,1,4,128,128]{4,3,2,1,0:T(8,128)(2,1)} %quant_hbm.1), custom_call_target="tpu_custom_call" | custom-call | flops 3300000000 | bytes 6000000 | tf_op jit(solution)/shard_map/completion_step/pallas_call | solution.py:393
  111.9 1.9 %copy.6 = f32[512,256]{1,0:T(8,128)} copy(f32[512,256]{1,0:T(8,128)} %completion_step.1) | data formatting | bytes 1048576

commit v3 on v2

--- a/solution.py
+++ b/solution.py
@@ -23,13 +23,20 @@
 OVER_Z = {1: (1, 7), 2: (1, 7, 2, 6), 3: (1, 7)}
 NEAR_Z = (1, 7, 2, 6)
 MESSAGES = 160
-LATE = 4
+OVER_T = (OVER_Z, OVER_Z)
+CHAIN = {4: 5, 5: 6, 6: 7, 7: 0, 3: 2, 2: 1, 1: 0}
+NEXT = (CHAIN, CHAIN)
+DURING = ((), (-2, -1, -3), (4, 3), ())
+AFTER = (
+    (1, 4), (1, 3), (0, 5), (0, 2), (1, -2), (1, -1), (1, -3), (1, 5),
+    (0, 6), (0, 1), (1, 2), (1, 6), (0, 7), (1, 1), (1, 7),
+)
 RING1, DENSE1, ZS = 2, 4, 3
 BF = jnp.bfloat16
 F32 = jnp.float32
 
 
-def index_rows(pattern):
+def index_rows(pattern, first):
     lane32 = lax.broadcasted_iota(jnp.int32, (GROUP, TILE), 1)
     sub32 = lax.broadcasted_iota(jnp.int32, (GROUP, TILE), 0)
     spread = jnp.zeros((GROUP, TILE), jnp.int32)
@@ -39,10 +46,12 @@
     full = (TILE, TILE)
     lane = lax.broadcasted_iota(jnp.int32, full, 1)
     sub = lax.broadcasted_iota(jnp.int32, full, 0)
+    turn = (sub - first) & (TILE - 1)
+    own_turn = (lane - first) & (TILE - 1)
     across = jnp.broadcast_to(flat, full)
     down = across.T
-    prev = jnp.max(jnp.where((across == down) & (sub < lane), sub, -1), axis=0, keepdims=True)
-    prev = jnp.where(prev < 0, NONE, prev)
+    prev = jnp.max(jnp.where((across == down) & (turn < own_turn), turn, -1), axis=0, keepdims=True)
+    prev = jnp.where(prev < 0, NONE, (prev + first) & (TILE - 1))
     held_down = jnp.max(jnp.where(across == sub, 1, 0), axis=1, keepdims=True)
     held_across = jnp.max(jnp.where(down == lane, 1, 0), axis=0, keepdims=True)
     before = ((lane >> 2) == (sub >> 2)) & (lane < sub)
@@ -52,15 +61,16 @@
     wanted = (jnp.broadcast_to(held_down, full) == 1) & (place == lane)
     need = jnp.sum(jnp.where(wanted, sub & 3, 0), axis=0, keepdims=True)
     slot_down = jnp.broadcast_to(slot, full).T
-    last = jnp.max(jnp.where(slot_down == lane, sub, -1), axis=0, keepdims=True)
-    last = jnp.where(last < 0, NONE, last)
+    last = jnp.max(jnp.where(slot_down == lane, turn, -1), axis=0, keepdims=True)
+    last = jnp.where(last < 0, NONE, (last + first) & (TILE - 1))
     return slot, prev, last, need
 
 
 def kernel(
-    pattern_ref, expo_ref, fac, quant_hbm, out_ref,
-    qraw, qs0, qs1, rowp, panel0, panel1, sums, racc, rsend, rrecv,
-    xs0, xs1, zp0, zp1, cs0, cs1, cr0, cr1, co0, co1, zs0, zs1, zr0, zr1, zown,
+    pattern_ref, expo_ref, fac_hbm, quant_hbm, out_ref,
+    fac, qraw, qs0, qs1, rowp, panel0, panel1, sums, racc, rsend, rrecv,
+    xs0, xs1, zp0, zp1, cs0, cs1, cr0, cr1, co0, co1, zs0, zs1, zr0, zr1,
+    zc0, zc1, zcr0, zcr1, cd0, cd1, ds0, ds1, dr0, dr1,
     idxv, idxs, nrv, nrs,
     *rest,
 ):
@@ -69,6 +79,7 @@
     qsem, isem, send_sem, recv_sem = rest[22:]
     qs, panel, xs, zp = (qs0, qs1), (panel0, panel1), (xs0, xs1), (zp0, zp1)
     cs, cr, co, zs, zr = (cs0, cs1), (cr0, cr1), (co0, co1), (zs0, zs1), (zr0, zr1)
+    zc, zcr, cd, ds, dr = (zc0, zc1), (zcr0, zcr1), (cd0, cd1), (ds0, ds1), (dr0, dr1)
     w = lax.axis_index("wide")
     n = lax.axis_index("narrow")
     x, z = lax.rem(w, NX), lax.div(w, NX)
@@ -91,23 +102,25 @@
     for peer in peers:
         pl.semaphore_signal(barrier, inc=1, device_id=peer, device_id_type=MESH)
 
+    grab = pltpu.make_async_copy(fac_hbm, fac, isem.at[2])
+    grab.start()
     fetch = pltpu.make_async_copy(quant_hbm, qraw, qsem)
     fetch.start()
-
+    grab.wait()
     for k in range(BLK):
         block = fac[k * TILE : (k + 1) * TILE, :].astype(BF)
         rowp[n * BLK + k] = block
         zb[0][0][k] = block[:HALF]
         zb[1][0][k] = block[HALF:]
+
+    first_row = lax.rem(y + 1, NY) * 8
     idxv[...] = jnp.zeros((8, TILE), jnp.int32)
     idxv[0:4, 0:GROUP] = pattern_ref[...]
-    rows = index_rows(idxv[...].T[:GROUP, :4])
+    rows = index_rows(idxv[...].T[:GROUP, :4], first_row * 4)
     for i, row in enumerate(rows):
         idxv[i : i + 1, :] = row
     spill = pltpu.make_async_copy(idxv, idxs, isem.at[0])
     spill.start()
-    sums[NONE] = jnp.zeros((HALF, RANK), F32)
-
     pl.semaphore_wait(barrier, len(peers))
     sent = []
     used = iter(range(MESSAGES))
@@ -153,6 +166,8 @@
     dense_send(0)
     mine = rowp.at[pl.ds(n * BLK, BLK)]
     row_in = [send(mine, mine, (w, n_peer(*s))) for s in narrow_steps]
+
+    sums[NONE] = jnp.zeros((HALF, RANK), F32)
 
     def owner(d, dx=0):
         return lax.rem(z + d, NZ) * NX + lax.rem(x + dx, NX)
@@ -207,9 +222,8 @@
                 ring_send(h, r + 1)
             if r == RING1 and h == 0:
                 ring_send(1, 1)
-            spread_along_x(h, (-r) % NZ)
-            if r < 4:
-                spread_along_x(h, r)
+            for d in ((-r) % NZ, r)[: 2 if r < 4 else 1]:
+                spread_along_x(h, d)
             if r == DENSE1 and h == 0:
                 dense_send(1)
             if r == ZS and r < 4:
@@ -238,7 +252,8 @@
         copy.wait_recv()
 
     def compute(h, low_row, high_row):
-        def step(b, carry):
+        def step(turn, carry):
+            b = lax.rem(first_row + turn, GROUP)
             mine = rowp[b]
             cols = jnp.concatenate([panel[h][idxs[0, b * 4 + t]] for t in range(4)], axis=0)
             pred = lax.dot_general(mine, cols, (((1,), (1,)), ((), ())), preferred_element_type=F32)
@@ -259,48 +274,110 @@
 
         lax.fori_loop(low_row, high_row, step, 0, unroll=4)
 
-    terms_in = {}
+    terms_in, near_in, dense_in, chain_in = {}, {}, {}, {}
+    near = [[(dx, d) for dx in (2, 1, 3) for d in OVER_T[h][dx]] for h in range(2)]
 
     def send_terms(h):
+        for p, (dx, d) in enumerate(near[h]):
+            at = owner(d, dx) * 2
+            for r in range(2):
+                zc[h][p, r] = sums[idxs[2, at + r]].astype(BF)
+            near_in[h, dx, d] = send(zc[h].at[p], zcr[h].at[p], z_peer(d))
         for d in FAR_FIRST:
             for dx in (2, 1, 3):
                 at = owner(d, dx) * 2
-                for r in range(2):
-                    cs[h][dx - 1, d, r] = sums[idxs[2, at + r]].astype(BF)
-                terms_in[h, d, dx] = send(cs[h].at[dx - 1, d], cr[h].at[dx - 1, d], x_peer(dx))
+                if d == 0 and OVER_T[h][dx]:
+                    for r in range(2):
+                        cd[h][dx - 1, r] = sums[idxs[2, at + r]]
+                elif d not in OVER_T[h][dx]:
+                    for r in range(2):
+                        cs[h][dx - 1, d, r] = sums[idxs[2, at + r]].astype(BF)
+                    terms_in[h, d, dx] = send(cs[h].at[dx - 1, d], cr[h].at[dx - 1, d], x_peer(dx))
             at = owner(d) * 2
             for r in range(2):
                 co[h][d, r] = sums[idxs[2, at + r]]
 
-    z_in = {0: [], 1: []}
-
-    def add_terms(h, d):
-        for dx in range(1, NX):
-            terms_in[h, d, dx].wait_recv()
-        at = owner(d) * 2
-        marks = []
-        for source in range(4):
-            for r in range(2):
-                place = idxs[3, at + r] if source == 0 else nrs[of_x[NX - source], 3, at + r]
-                marks.append([jnp.where(place == k, 1.0, 0.0).astype(F32) for k in range(BLK)])
+    def combine(pairs, wholes, write):
+        marks = [
+            [[jnp.where(place == k, 1.0, 0.0).astype(F32) for k in range(BLK)] for place in places]
+            for _, places in pairs
+        ]
 
         def strip(i, carry):
             span = pl.ds(pl.multiple_of(i * 16, 16), 16)
-            terms = [co[h][d, r, span, :] for r in range(2)]
-            terms += [cr[h][source, d, r, span, :].astype(F32) for source in range(3) for r in range(2)]
+            terms = [load(r, span).astype(F32) for load, _ in pairs for r in range(2)]
+            flat = [mark for pair in marks for mark in pair]
             for k in range(BLK):
-                total = terms[0] * marks[0][k]
-                for term, mark in zip(terms[1:], marks[1:]):
+                total = terms[0] * flat[0][k]
+                for term, mark in zip(terms[1:], flat[1:]):
                     total = total + term * mark[k]
-                if d == 0:
-                    zown[h, k, span, :] = total
-                else:
-                    zs[h][d - 1, k, span, :] = total.astype(BF)
+                for whole in wholes:
+                    total = total + whole[k, span, :].astype(F32)
+                write(k, i, span, total)
             return carry
 
         lax.fori_loop(0, HALF // 16, strip, 0)
+
+    def own_places(at):
+        return [idxs[3, at + r] for r in range(2)]
+
+    def peer_places(j, at):
+        return [nrs[j, 3, at + r] for r in range(2)]
+
+    def add_near(h, dx):
+        if not OVER_T[h][dx]:
+            return
+        at = owner(0, dx) * 2
+        pairs = [(lambda r, span: cd[h][dx - 1, r, span, :], own_places(at))]
+        for p, (dx_p, d) in enumerate(near[h]):
+            if dx_p == dx:
+                near_in[h, dx, d].wait_recv()
+                pairs.append(
+                    (lambda r, span, p=p: zcr[h][p, r, span, :], peer_places(of_z[NZ - d], at))
+                )
+
+        def write(k, i, span, total):
+            ds[h][dx - 1, k, span, :] = total.astype(BF)
+
+        combine(pairs, [], write)
+        dense_in[h, dx] = send(ds[h].at[dx - 1], dr[h].at[dx - 1], x_peer(dx))
+
+    def add_terms(h, d):
+        at = owner(d) * 2
+        pairs = [(lambda r, span: co[h][d, r, span, :], own_places(at))]
+        wholes = []
+        for dx in range(1, NX):
+            if d == 0 and OVER_T[h][dx]:
+                dense_in[h, dx].wait_recv()
+                wholes.append(dr[h].at[dx - 1])
+            elif d not in OVER_T[h][dx]:
+                terms_in[h, d, dx].wait_recv()
+                pairs.append(
+                    (lambda r, span, dx=dx: cr[h][dx - 1, d, r, span, :], peer_places(of_x[NX - dx], at))
+                )
+        for came in (e for e in FAR_FIRST if e != 0 and NEXT[h][e] == d):
+            chain_in[h, came].wait_recv()
+            wholes.append(zr[h].at[came - 1])
+
+        def write(k, i, span, total):
+            if d == 0:
+                outer = pl.ds(pl.multiple_of(k * TILE + h * HALF + i * 16, 16), 16)
+                out_ref[outer, :] = out_ref[outer, :] - step_rate * total
+            else:
+                zs[h][d - 1, k, span, :] = total.astype(BF)
+
+        combine(pairs, wholes, write)
         if d != 0:
-            z_in[h].append(send(zs[h].at[d - 1], zr[h].at[d - 1], z_peer(d)))
+            chain_in[h, d] = send(zs[h].at[d - 1], zr[h].at[d - 1], z_peer((d - NEXT[h][d]) % NZ))
+
+    r_in = []
+
+    def send_rows(dy):
+        for c_step in range(NC):
+            if (dy, c_step) != (0, 0):
+                j = narrow_steps.index((dy, c_step))
+                peer = n_peer(dy, c_step)
+                r_in.append(send(rsend.at[pl.ds(peer * BLK, BLK)], rrecv.at[j], (w, peer)))
 
     for copy in panel_in[0]:
         copy.wait_recv()
@@ -308,26 +385,16 @@
     send_terms(0)
     for copy in panel_in[1]:
         copy.wait_recv()
-    early = len(FAR_FIRST) - LATE
     for part in range(4):
         compute(1, part * 8, part * 8 + 8)
-        if part >= 4 - early:
-            add_terms(0, FAR_FIRST[part - 4 + early])
+        send_rows((part + 1) % NY)
+        for job in DURING[part]:
+            add_near(0, -job) if job < 0 else add_terms(0, job)
     send_terms(1)
-    r_in = [
-        send(rsend.at[pl.ds(n_peer(*s) * BLK, BLK)], rrecv.at[j], (w, n_peer(*s)))
-        for j, s in enumerate(narrow_steps)
-    ]
-    for d in FAR_FIRST[early:]:
-        add_terms(0, d)
-    for d in FAR_FIRST[:-3]:
-        add_terms(1, d)
+    for h, job in AFTER:
+        add_near(h, -job) if job < 0 else add_terms(h, job)
     for copy in r_in:
         copy.wait_recv()
-    settled = sent[-3:]
-    del sent[-3:]
-    settle()
-    sent.extend(settled)
 
     def base(i, carry):
         for k in range(BLK):
@@ -340,26 +407,8 @@
         return carry
 
     lax.fori_loop(0, TILE // 16, base, 0)
-    for d in FAR_FIRST[-3:]:
-        add_terms(1, d)
-
-    def finish(h):
-        def strip(i, carry):
-            for k in range(BLK):
-                span = pl.ds(pl.multiple_of(i * 16, 16), 16)
-                outer = pl.ds(pl.multiple_of(k * TILE + h * HALF + i * 16, 16), 16)
-                total = zown[h, k, span, :]
-                for j in range(7):
-                    total = total + zr[h][j, k, span, :].astype(F32)
-                out_ref[outer, :] = out_ref[outer, :] - step_rate * total
-            return carry
-
-        for copy in z_in[h]:
-            copy.wait_recv()
-        lax.fori_loop(0, HALF // 16, strip, 0)
-
-    finish(0)
-    finish(1)
+    add_terms(0, 0)
+    add_terms(1, 0)
     settle()
 
 
@@ -369,6 +418,7 @@
     dma = pltpu.SemaphoreType.DMA
     V = pltpu.VMEM
     scratch = [
+        V(factor.shape, F32),
         V((GROUP, 1, 4, TILE, TILE), BF),
         V((GROUP, 2, TILE, TILE), BF), V((GROUP, 2, TILE, TILE), BF),
         V((GROUP, TILE, RANK), BF),
@@ -383,17 +433,19 @@
     scratch += [V((3, NZ, 2, HALF, RANK), BF)] * 4
     scratch += [V((NZ, 2, HALF, RANK), F32)] * 2
     scratch += [V((7, BLK, HALF, RANK), BF)] * 4
-    scratch += [V((2, BLK, HALF, RANK), F32)]
+    scratch += [V((8, 2, HALF, RANK), BF)] * 4
+    scratch += [V((3, 2, HALF, RANK), F32)] * 2
+    scratch += [V((3, BLK, HALF, RANK), BF)] * 4
     scratch += [
         V((8, TILE), jnp.int32), pltpu.SMEM((8, TILE), jnp.int32),
         V((7, 8, TILE), jnp.int32), pltpu.SMEM((7, 8, TILE), jnp.int32),
     ]
     scratch += [V((BLK, HALF, RANK), BF)] * 22
-    scratch += [dma, dma((2,)), dma((MESSAGES,)), dma((MESSAGES,))]
+    scratch += [dma, dma((3,)), dma((MESSAGES,)), dma((MESSAGES,))]
     return pl.pallas_call(
         kernel,
         out_shape=jax.ShapeDtypeStruct(factor.shape, factor.dtype),
-        in_specs=[vmem, smem, vmem, pl.BlockSpec(memory_space=pl.ANY)],
+        in_specs=[vmem, smem, pl.BlockSpec(memory_space=pl.ANY), pl.BlockSpec(memory_space=pl.ANY)],
         out_specs=vmem,
         scratch_shapes=scratch,
         compiler_params=pltpu.CompilerParams(

time: 115 us -> 109 us (0.948); the launches traced: 114 us -> 109 us
  Pallas kernels: 112 us -> 107 us
    pallas_call x1, Pallas kernels: 112 us -> 107 us  [body(): pl.pallas_call(kernel, out_shape=jax.ShapeDtypeStruct(factor.shape, facto...]
where the time goes in v3:
time: 109 us
  Pallas kernels  107 us (98%)
  local copies, waits for them, and re-layouts  1.87 us (2%)
    pallas_call x1, Pallas kernels, body(): pl.pallas_call(kernel, out_shape=jax.ShapeDtypeStruct(factor.shape, facto...  107 us

profile of v3, /device:TPU:8, one launch (start us, length us, event | category | flops | bytes accessed | tf_op | source)
XLA Modules:
  0.0 109.1 jit_solution(13111026738331797484)
XLA Ops:
  0.0 107.2 %completion_step.1 = f32[512,256]{1,0:T(8,128)} custom-call(s32[4,32]{1,0:T(4,128)} %bitcast.6, s32[4,32]{1,0:T(4,128)} %bitcast.7, f32[512,256]{1,0:T(8,128)} %fac_hbm.1, bf16[32,1,4,128,128]{4,3,2,1,0:T(8,128)(2,1)} %quant_hbm.1), custom_call_target="tpu_custom_call" | custom-call | flops 3300000000 | bytes 6000000 | tf_op jit(solution)/shard_map/completion_step/pallas_call | solution.py:445
  107.2 1.9 %copy.6 = f32[512,256]{1,0:T(8,128)} copy(f32[512,256]{1,0:T(8,128)} %completion_step.1) | data formatting | bytes 1048576

commit v4 on v3

--- a/solution.py
+++ b/solution.py
@@ -26,10 +26,9 @@
 OVER_T = (OVER_Z, OVER_Z)
 CHAIN = {4: 5, 5: 6, 6: 7, 7: 0, 3: 2, 2: 1, 1: 0}
 NEXT = (CHAIN, CHAIN)
-DURING = ((), (-2, -1, -3), (4, 3), ())
 AFTER = (
-    (1, 4), (1, 3), (0, 5), (0, 2), (1, -2), (1, -1), (1, -3), (1, 5),
-    (0, 6), (0, 1), (1, 2), (1, 6), (0, 7), (1, 1), (1, 7),
+    (0, 4), (0, 3), (0, -2), (0, -1), (0, -3), (1, 4), (1, 3), (0, 5), (0, 2), (1, -2), (1, -1), (1, -3),
+    (1, 5), (0, 6), (0, 1), (1, 2), (1, 6), (0, 7), (1, 1), (1, 7),
 )
 RING1, DENSE1, ZS = 2, 4, 3
 BF = jnp.bfloat16
@@ -388,8 +387,6 @@
     for part in range(4):
         compute(1, part * 8, part * 8 + 8)
         send_rows((part + 1) % NY)
-        for job in DURING[part]:
-            add_near(0, -job) if job < 0 else add_terms(0, job)
     send_terms(1)
     for h, job in AFTER:
         add_near(h, -job) if job < 0 else add_terms(h, job)

time: 109 us -> 106 us (0.972)
  Pallas kernels: 107 us -> 104 us
    pallas_call x1, Pallas kernels: 107 us -> 104 us  [body(): pl.pallas_call(kernel, out_shape=jax.ShapeDtypeStruct(factor.shape, facto...]
where the time goes in v4:
time: 106 us
  Pallas kernels  104 us (98%)
  local copies, waits for them, and re-layouts  1.87 us (2%)
    pallas_call x1, Pallas kernels, body(): pl.pallas_call(kernel, out_shape=jax.ShapeDtypeStruct(factor.shape, facto...  104 us

profile of v4, /device:TPU:8, one launch (start us, length us, event | category | flops | bytes accessed | tf_op | source)
XLA Modules:
  0.0 106.0 jit_solution(9302602934175031456)
XLA Ops:
  0.0 104.2 %completion_step.1 = f32[512,256]{1,0:T(8,128)} custom-call(s32[4,32]{1,0:T(4,128)} %bitcast.6, s32[4,32]{1,0:T(4,128)} %bitcast.7, f32[512,256]{1,0:T(8,128)} %fac_hbm.1, bf16[32,1,4,128,128]{4,3,2,1,0:T(8,128)(2,1)} %quant_hbm.1), custom_call_target="tpu_custom_call" | custom-call | flops 3300000000 | bytes 6000000 | tf_op jit(solution)/shard_map/completion_step/pallas_call | solution.py:442
  104.2 1.9 %copy.6 = f32[512,256]{1,0:T(8,128)} copy(f32[512,256]{1,0:T(8,128)} %completion_step.1) | data formatting | bytes 1048576
